TPU v7x, 256 devices: a whole 4x4x8 slice. The times are simulated.
256 devices in a mesh: freq: 2 (over core), inl: 16 (over y, x), xl: 8 (over z).
Axes of the slice: x: 4, y: 4, z: 8, core: 2. Of those that a mesh axis runs over, the one named last changes fastest.
Arguments:
- spectra: float32 [2, 2, 256, 1024], P('freq', None, 'inl', 'xl'), parts along dimension 0, may hold values from -6 to 6
- omega: float32 [2, 289, 64], replicated, may hold values from -0.25 to 0.25
Outputs:
- sketch: float32 [2, 128, 256, 1024], P('freq', None, 'inl', 'xl'), parts along dimension 0
- denoised: float32 [2, 2, 256, 1024], P('freq', None, 'inl', 'xl'), parts along dimension 0
There are 2 independent parts, one for each index of `freq`. A program takes and returns all parts, laid end to end along the dimension named above; an argument that names none is the same for every part. Nothing has to cross between parts.
All inputs are finite; a program needn't handle non-finite values.
Results may differ from a plain program's by a relative error of at most 0.0001.
Values sent between devices are 32-bit elements; how exact they have to be, the bound alone decides.
A program may use at most 64 MiB of HBM per device.

v0:
```python
import functools

import jax
import jax.numpy as jnp
from jax import lax
from jax.experimental import pallas as pl
from jax.experimental.pallas import tpu as pltpu
from jax.sharding import PartitionSpec as P

MESH = pl.DeviceIdType.MESH
F32 = jnp.float32
BF16 = jnp.bfloat16
KI = 17
HW = 8
WIN = 24
GROUPS = 2 * KI
KROWS = GROUPS * WIN
KPAD = 896
TROWS = 384
LANES = 128
CH = 128
HALF = 64


def split(value):
    high = value.astype(BF16)
    return high, (value - high.astype(F32)).astype(BF16)


def mm(a, b):
    return jnp.dot(a, b, preferred_element_type=F32)


def mm_exact(a, b):
    return jnp.dot(a, b, preferred_element_type=F32, precision=lax.Precision.HIGHEST)


def mm_t(a, b):
    return lax.dot_general(a, b, (((1,), (1,)), ((), ())), preferred_element_type=F32)


def roll(value, amount, axis=1):
    size = value.shape[axis]
    amount = amount % size
    return value if amount == 0 else pltpu.roll(value, amount, axis)


def lane_iota(rows, lanes=LANES):
    return lax.broadcasted_iota(jnp.int32, (rows, lanes), 1)


def prepare_weights(omega_ref, taps_ref, compact_ref, band_hi, band_lo):
    taps_ref[...] = jnp.zeros_like(taps_ref)
    taps_ref[0 : KI * KI, :] = jnp.concatenate([omega_ref[0], omega_ref[1]], axis=1)
    taps = taps_ref[...]
    tap_t = taps.T
    turned = jnp.concatenate([-tap_t[HALF:], tap_t[:HALF]], axis=0)
    col = lane_iota(1, KPAD)
    second = col >= KROWS // 2
    inner = jnp.where(second, col - KROWS // 2, col)
    q = (inner * 2731) >> 16
    r = inner - q * WIN
    tap = jnp.where((r < KI) & (col < KROWS), r * KI + q, -1)
    row = lax.broadcasted_iota(jnp.int32, (TROWS, KPAD), 0)
    pick_re = (row == jnp.where(second, -1, tap)).astype(F32).astype(BF16)
    pick_im = (row == jnp.where(second, tap, -1)).astype(F32).astype(BF16)
    re_hi, re_lo = split(tap_t)
    im_hi, im_lo = split(turned)
    wide_hi = mm(re_hi, pick_re) + mm(im_hi, pick_im)
    wide_lo = mm(re_lo, pick_re) + mm(im_lo, pick_im)
    for shift in range(8):
        band_hi[shift * CH : (shift + 1) * CH, :] = roll(wide_hi, shift).astype(BF16)
        band_lo[shift * CH : (shift + 1) * CH, :] = roll(wide_lo, shift).astype(BF16)
    m = lax.broadcasted_iota(jnp.int32, (TROWS, TROWS), 0)
    tap = jnp.where(m < 272, (m & 15) * KI + (m >> 4), jnp.where(m < 289, 16 * KI + m - 272, -1))
    pick = (lane_iota(TROWS, TROWS) == tap).astype(F32)
    compact_ref[...] = mm_exact(pick, taps)


def shifted(left, centre, right, s, lane):
    if s == 0:
        return centre
    if s < 0:
        return jnp.where(lane < -s, roll(left, -s), roll(centre, -s))
    return jnp.where(lane >= LANES - s, roll(right, LANES - s), roll(centre, LANES - s))


def plane(block_ref, x, dc):
    return jnp.concatenate([block_ref[dr, dc, x] for dr in range(3)], axis=0)


def build_main(block_ref, s_hi, s_lo):
    lane = lane_iota(48)
    windows = []
    for x in range(2):
        left, centre, right = (plane(block_ref, x, dc) for dc in range(3))
        for q in range(KI):
            windows.append(shifted(left, centre, right, q - HW, lane))
    for k in range(KI):
        first, second = windows[2 * k], windows[2 * k + 1]
        for g in range(4):
            value = jnp.concatenate([first[8 * g : 8 * g + WIN], second[8 * g : 8 * g + WIN]], axis=0)
            high, low = split(value)
            s_hi[48 * k : 48 * k + 48, g * LANES : (g + 1) * LANES] = high
            s_lo[48 * k : 48 * k + 48, g * LANES : (g + 1) * LANES] = low


def build_side(block_ref, s_hi, s_lo):
    lane = lane_iota(48)
    strips = []
    for x in range(2):
        left, centre, right = (plane(block_ref, x, dc) for dc in range(3))
        for q in range(KI):
            inner = roll(centre, 16 - q)
            near = lane < 16 - q
            strip = jnp.where(
                lane < 8,
                jnp.where(near, roll(left, 16 - q), inner),
                jnp.where(near, inner, roll(right, 16 - q)),
            )
            strip = jnp.where(lane < 16, strip, 0.0)
            total = strip[0:WIN]
            for g in range(1, 4):
                total = total + roll(strip[8 * g : 8 * g + WIN], 16 * g)
            strips.append(total)
    for k in range(KI):
        high, low = split(jnp.concatenate([strips[2 * k], strips[2 * k + 1]], axis=0))
        s_hi[48 * k : 48 * k + 48, 512:640] = high
        s_lo[48 * k : 48 * k + 48, 512:640] = low


def invert(t):
    lane = lane_iota(HALF)
    sub = lax.broadcasted_iota(jnp.int32, (HALF, LANES), 0)
    lane_row = lane_iota(1)
    for k in range(HALF):
        pivot = 1.0 / t[k : k + 1, k : k + 1]
        row = t[k : k + 1, :]
        row = jnp.where(lane_row == k, 1.0, jnp.where(lane_row == HALF + k, 0.0, row)) * pivot
        other = jnp.where(lane_row < HALF, -roll(row, HALF), roll(row, HALF))
        here = sub == k
        real = jnp.where(here, -1.0, t[:, k : k + 1])
        imag = jnp.where(here, 0.0, t[:, HALF + k : HALF + k + 1])
        kept = jnp.where(here | (lane == k) | (lane == HALF + k), 0.0, t)
        t = kept - real * row - imag * other
    return t


def counts(start, length, total, index):
    at = start + index
    return (jnp.minimum(at + HW, total - 1) - jnp.maximum(at - HW, 0) + 1).astype(F32)


def kernel(
    n_inl,
    n_xl,
    spectra_ref,
    omega_ref,
    sketch_out,
    denoised_ref,
    block_ref,
    taps_ref,
    compact_ref,
    band_hi,
    band_lo,
    s_hi,
    s_lo,
    y_hi,
    y_lo,
    sketch_ref,
    prod_ref,
    send_ref,
    recv_a,
    part_ref,
    recv_b,
    full_ref,
    recv_c,
    spread_ref,
    c_hi,
    c_lo,
    halo_send,
    halo_recv,
    a_send,
    a_recv,
    b_send,
    b_recv,
    c_send,
    c_recv,
    out_sem,
):
    inl = lax.axis_index("inl")
    xl = lax.axis_index("xl")
    share = TROWS // n_inl

    up, down = inl > 0, inl < n_inl - 1
    west, east = xl > 0, xl < n_xl - 1
    barrier = pltpu.get_barrier_semaphore()
    sides = [(dr, dc) for dr in (-1, 0, 1) for dc in (-1, 0, 1) if (dr, dc) != (0, 0)]

    def exists(dr, dc):
        ok = None
        for step, low, high in ((dr, up, down), (dc, west, east)):
            if step != 0:
                one = low if step < 0 else high
                ok = one if ok is None else ok & one
        return ok

    for k in range(1, n_inl):
        pl.semaphore_signal(
            barrier, inc=1, device_id={"inl": lax.rem(inl + k, n_inl)}, device_id_type=MESH
        )
    for k in range(1, n_xl):
        pl.semaphore_signal(
            barrier, inc=1, device_id={"xl": lax.rem(xl + k, n_xl)}, device_id_type=MESH
        )
    expected = n_inl - 1 + n_xl - 1
    for dr, dc in sides:
        if dr != 0 and dc != 0:
            there = exists(dr, dc)
            expected = expected + there.astype(jnp.int32)

            @pl.when(there)
            def _(dr=dr, dc=dc):
                pl.semaphore_signal(
                    barrier, inc=1, device_id={"inl": inl + dr, "xl": xl + dc}, device_id_type=MESH
                )

    s_hi[KROWS:KPAD, :] = jnp.zeros((KPAD - KROWS, 640), BF16)
    s_lo[KROWS:KPAD, :] = jnp.zeros((KPAD - KROWS, 640), BF16)
    pl.semaphore_wait(barrier, expected)

    def halo(n, dr, dc):
        return pltpu.make_async_remote_copy(
            src_ref=spectra_ref,
            dst_ref=block_ref.at[1 - dr, 1 - dc],
            send_sem=halo_send.at[n],
            recv_sem=halo_recv.at[n],
            device_id={"inl": inl + dr, "xl": xl + dc},
            device_id_type=MESH,
        )

    for n, (dr, dc) in enumerate(sides):

        @pl.when(exists(dr, dc))
        def _(n=n, dr=dr, dc=dc):
            halo(n, dr, dc).start()

    for dr, dc in sides:

        @pl.when(jnp.logical_not(exists(dr, dc)))
        def _(dr=dr, dc=dc):
            block_ref[1 + dr, 1 + dc] = jnp.zeros((2, 16, LANES), F32)

    block_ref[1, 1] = spectra_ref[...]

    prepare_weights(omega_ref, taps_ref, compact_ref, band_hi, band_lo)

    for n, (dr, dc) in enumerate(sides):

        @pl.when(exists(dr, dc))
        def _(n=n, dr=dr, dc=dc):
            halo(n, dr, dc).wait_send()

        @pl.when(exists(-dr, -dc))
        def _(n=n, dr=dr, dc=dc):
            halo(n, dr, dc).wait_recv()

    build_main(block_ref, s_hi, s_lo)

    def sketch_rows(shift, at, width):
        rows = slice(shift * CH, (shift + 1) * CH)
        left_hi = band_hi[rows, :]
        right = s_hi[:, at : at + width]
        return mm(left_hi, right) + mm(band_lo[rows, :], right) + mm(left_hi, s_lo[:, at : at + width])

    for shift in range(8):
        value = sketch_rows(shift, LANES, 2 * LANES)
        for half in range(2):
            sketch_ref[pl.ds(8 * half + shift, CH, stride=16), :] = value[
                :, half * LANES : (half + 1) * LANES
            ]
        high, low = split(value)
        y_hi[shift * CH : (shift + 1) * CH, 128:384] = high
        y_lo[shift * CH : (shift + 1) * CH, 128:384] = low

    copy_out = pltpu.make_async_copy(sketch_ref, sketch_out, out_sem)
    copy_out.start()

    main_hi, main_lo = s_hi[0:KROWS, 128:384], s_lo[0:KROWS, 128:384]
    prod_ref[KROWS : KROWS + 8, :] = jnp.zeros((8, 256), F32)
    total = None
    for pair in range(4):
        rows = slice(pair * 256, (pair + 1) * 256)
        own_hi = y_hi[rows, 128:384]
        prod_ref[0:KROWS, :] = (
            mm_t(main_hi, own_hi) + mm_t(main_lo, own_hi) + mm_t(main_hi, y_lo[rows, 128:384])
        )
        for k in range(2):
            term = prod_ref[2 * pair + k : 2 * pair + k + KROWS, k * LANES : (k + 1) * LANES]
            total = term if total is None else total + term
    prod_ref[0:KROWS, 0:LANES] = total
    first = prod_ref[0 : KROWS // 2, 0:LANES]
    second = prod_ref[KROWS // 2 : KROWS, 0:LANES]
    sign = jnp.where(lane_iota(1) < HALF, 1.0, -1.0)
    moments = roll(second, HALF) + first * sign
    for q in range(KI):
        send_ref[q * 16 : q * 16 + 16, :] = moments[q * WIN : q * WIN + 16]
        send_ref[272 + q : 273 + q, :] = moments[q * WIN + 16 : q * WIN + 17]
    send_ref[289:TROWS, :] = jnp.zeros((TROWS - 289, LANES), F32)

    def piece(at):
        return pl.ds(pl.multiple_of(at * share, 8), share)

    def scatter(k):
        peer = lax.rem(inl + k, n_inl)
        return pltpu.make_async_remote_copy(
            src_ref=send_ref.at[piece(peer)],
            dst_ref=recv_a.at[inl],
            send_sem=a_send.at[k],
            recv_sem=a_recv.at[k],
            device_id={"inl": peer},
            device_id_type=MESH,
        )

    def across(k):
        return pltpu.make_async_remote_copy(
            src_ref=part_ref,
            dst_ref=recv_b.at[xl],
            send_sem=b_send.at[k],
            recv_sem=b_recv.at[k],
            device_id={"xl": lax.rem(xl + k, n_xl)},
            device_id_type=MESH,
        )

    def gather(k):
        return pltpu.make_async_remote_copy(
            src_ref=full_ref,
            dst_ref=recv_c.at[inl],
            send_sem=c_send.at[k],
            recv_sem=c_recv.at[k],
            device_id={"inl": lax.rem(inl + k, n_inl)},
            device_id_type=MESH,
        )

    for k in range(1, n_inl):
        scatter(k).start()
    recv_a[inl] = send_ref[piece(inl), :]

    build_side(block_ref, s_hi, s_lo)
    side_lane = lane_iota(1)
    keep_up = up.astype(F32)
    keep_down = down.astype(F32)
    keep_side = jnp.where(side_lane % 16 < 8, west.astype(F32), east.astype(F32))
    keep = jnp.concatenate([jnp.full((1, LANES), keep_down), keep_side], axis=1)
    for shift in range(8):
        rows = slice(shift * CH, (shift + 1) * CH)
        high, low = split(sketch_rows(shift, 0, LANES) * keep_up)
        y_hi[rows, 0:128] = high
        y_lo[rows, 0:128] = low
        value = sketch_rows(shift, 384, 256)
        side = value[:, LANES:]
        side_keep = jnp.where(
            side_lane < 16, keep_up, jnp.where((side_lane >= 48) & (side_lane < 64), keep_down, 1.0)
        )
        high, low = split(value * keep * jnp.concatenate([jnp.ones((1, LANES), F32), side_keep], axis=1))
        y_hi[rows, 384:640] = high
        y_lo[rows, 384:640] = low

    for k in range(1, n_inl):
        scatter(k).wait()
    value = recv_a[0]
    for k in range(1, n_inl):
        value = value + recv_a[k]
    part_ref[...] = value
    for k in range(1, n_xl):
        across(k).start()
    recv_b[xl] = value
    for k in range(1, n_xl):
        across(k).wait()
    value = recv_b[0]
    for k in range(1, n_xl):
        value = value + recv_b[k]
    full_ref[...] = value
    for k in range(1, n_inl):
        gather(k).start()
    recv_c[inl] = value
    for k in range(1, n_inl):
        gather(k).wait()

    moments = recv_c[...].reshape(TROWS, LANES)
    products = mm_exact(moments.T, compact_ref[...])
    gram = products[:HALF] - roll(products[HALF:], HALF) * sign
    inverse = invert(gram)
    mixing = jnp.concatenate([inverse * sign, roll(inverse, HALF)], axis=0)
    coeffs = mm_exact(moments, mixing)

    spread_ref[:, 0:8, :] = jnp.zeros((GROUPS, 8, LANES), F32)
    spread_ref[:, 24:32, :] = jnp.zeros((GROUPS, 8, LANES), F32)
    for x, value in enumerate((coeffs * sign, roll(coeffs, HALF))):
        for q in range(KI):
            spread_ref[x * KI + q, 8:24, :] = value[q * 16 : q * 16 + 16]
            spread_ref[x * KI + q, 24:25, :] = value[272 + q : 273 + q]

    main = None
    edge = None
    for window in range(3):
        for shift in range(8):
            at = 8 + 8 * window - shift
            value = spread_ref[:, at : at + 8, :].reshape(GROUPS * 8, LANES)
            high, low = split(value)
            c_hi[:, shift * LANES : (shift + 1) * LANES] = high
            c_lo[:, shift * LANES : (shift + 1) * LANES] = low
        high, low = c_hi[...], c_lo[...]
        at = (2 - window) * LANES
        y = y_hi[:, at : at + 256]
        term = mm(high, y) + mm(low, y) + mm(high, y_lo[:, at : at + 256])
        main = term if main is None else main + term
        y = y_hi[:, 512:640]
        term = mm(high, y) + mm(low, y) + mm(high, y_lo[:, 512:640])
        term = roll(term, 16 * (window - 2))
        edge = term if edge is None else edge + term

    lane = lane_iota(8)
    sub = lax.broadcasted_iota(jnp.int32, (8, LANES), 0)
    count_j = counts(xl * LANES, LANES, n_xl * LANES, lane)
    for x in range(2):
        for h in range(2):
            total = None
            for q in range(KI):
                s = q - HW
                rows = slice((x * KI + q) * 8, (x * KI + q) * 8 + 8)
                value = roll(main[rows, h * LANES : (h + 1) * LANES], s)
                if s != 0:
                    outer = roll(edge[rows, :], s - 8 - 16 * h)
                    value = jnp.where(lane < s if s > 0 else lane >= LANES + s, outer, value)
                total = value if total is None else total + value
            count_i = counts(inl * 16 + 8 * h, 16, n_inl * 16, sub)
            denoised_ref[x, 8 * h : 8 * h + 8, :] = total / (count_i * count_j)

    copy_out.wait()


def per_device(n_inl, n_xl, spectra, omega):
    share = TROWS // n_inl
    vmem = pltpu.VMEM
    dma = pltpu.SemaphoreType.DMA
    sketch, denoised = pl.pallas_call(
        functools.partial(kernel, n_inl, n_xl),
        out_shape=(
            jax.ShapeDtypeStruct((CH * 16, LANES), F32),
            jax.ShapeDtypeStruct((2, 16, LANES), F32),
        ),
        in_specs=[pl.BlockSpec(memory_space=pltpu.VMEM)] * 2,
        out_specs=(pl.BlockSpec(memory_space=pl.ANY), pl.BlockSpec(memory_space=pltpu.VMEM)),
        scratch_shapes=[
            vmem((3, 3, 2, 16, LANES), F32),
            vmem((TROWS, LANES), F32),
            vmem((TROWS, LANES), F32),
            vmem((8 * CH, KPAD), BF16),
            vmem((8 * CH, KPAD), BF16),
            vmem((KPAD, 640), BF16),
            vmem((KPAD, 640), BF16),
            vmem((8 * CH, 640), BF16),
            vmem((8 * CH, 640), BF16),
            vmem((CH * 16, LANES), F32),
            vmem((KROWS + 8, 256), F32),
            vmem((TROWS, LANES), F32),
            vmem((n_inl, share, LANES), F32),
            vmem((share, LANES), F32),
            vmem((n_xl, share, LANES), F32),
            vmem((share, LANES), F32),
            vmem((n_inl, share, LANES), F32),
            vmem((GROUPS, 32, LANES), F32),
            vmem((GROUPS * 8, 8 * LANES), BF16),
            vmem((GROUPS * 8, 8 * LANES), BF16),
            dma((8,)),
            dma((8,)),
            dma((n_inl,)),
            dma((n_inl,)),
            dma((n_xl,)),
            dma((n_xl,)),
            dma((n_inl,)),
            dma((n_inl,)),
            dma,
        ],
        compiler_params=pltpu.CompilerParams(
            collective_id=0, has_side_effects=True, vmem_limit_bytes=48 * 1024 * 1024
        ),
    )(spectra[0], omega)
    return sketch.reshape(1, CH, 16, LANES), denoised[None]


def solution(mesh):
    in_specs = (P("freq", None, "inl", "xl"), P())
    out_specs = (P("freq", None, "inl", "xl"), P("freq", None, "inl", "xl"))
    return jax.shard_map(
        functools.partial(per_device, mesh.shape["inl"], mesh.shape["xl"]),
        mesh=mesh,
        in_specs=in_specs,
        out_specs=out_specs,
        check_vma=False,
    )
```

profile of v0, /device:TPU:8, one launch (start us, length us, event | category | flops | bytes accessed | tf_op | source)
XLA Modules:
  0.0 52.0 jit_solution(3488708756709510560)
XLA Ops:
  0.6 0.0 copy-start
  0.6 1.1 %copy.4.omega_ref = f32[2,289,64]{2,1,0:T(8,128)S(1)} copy(f32[2,289,64]{1,2,0:T(8,128)} %param.3) | data formatting | bytes 295936 | tf_op args[1]
  1.7 0.0 copy-done
  1.7 48.7 %shard_map.41 = (f32[2048,128]{1,0:T(8,128)S(1)}, f32[2,16,128]{2,1,0:T(8,128)S(1)}) custom-call(f32[2,16,128]{2,1,0:T(8,128)S(1)} %bitcast.4, f32[2,289,64]{2,1,0:T(8,128)S(1)} %copy.4.omega_ref), custom_call_target="tpu_custom_call" | custom-call | tf_op jit(solution)/shard_map/pallas_call | solution.py:447
  50.4 1.0 %copy.7 = f32[1,128,16,128]{3,2,1,0:T(8,128)} copy(f32[1,128,16,128]{3,2,1,0:T(8,128)S(1)} %bitcast.3) | data formatting | bytes 2097152
  51.4 0.6 %copy.8 = f32[1,2,16,128]{3,2,1,0:T(8,128)} copy(f32[1,2,16,128]{3,2,1,0:T(8,128)S(1)} %bitcast.5) | data formatting | bytes 32768
Async XLA Ops:
  0.6 1.1 %copy-start = (f32[1,2,16,128]{3,2,1,0:T(8,128)S(1)}, f32[1,2,16,128]{3,2,1,0:T(8,128)}, u32[]{:S(2)}) copy-start(f32[1,2,16,128]{3,2,1,0:T(8,128)} %param.2) | copy-start | bytes 49156
where the time goes:
time: 52.1 us; the launch traced here: 52 us
  Pallas kernels  48.7 us (93%)
  local copies, waits for them, and re-layouts  2.66 us (5%)
  between operations  0.66 us (1%)
    pallas_call x1, Pallas kernels, per_device(): pl.pallas_call(functools.partial(kernel, n_inl, n_xl), out_shape=(jax.Sha...  48.7 us
    unnamed x5, local copies, waits for them, and re-layouts  2.66 us

commit v1 on v0

--- a/solution.py
+++ b/solution.py
@@ -49,11 +49,11 @@
     return lax.broadcasted_iota(jnp.int32, (rows, lanes), 1)
 
 
-def prepare_weights(omega_ref, taps_ref, compact_ref, band_hi, band_lo):
-    taps_ref[...] = jnp.zeros_like(taps_ref)
-    taps_ref[0 : KI * KI, :] = jnp.concatenate([omega_ref[0], omega_ref[1]], axis=1)
-    taps = taps_ref[...]
-    tap_t = taps.T
+def prepare_weights(omega_ref, taps_ref, band_hi, band_lo):
+    taps_ref[:, 256:TROWS] = jnp.zeros((CH, TROWS - 256), F32)
+    taps_ref[0:HALF, 0 : KI * KI] = omega_ref[0]
+    taps_ref[HALF:CH, 0 : KI * KI] = omega_ref[1]
+    tap_t = taps_ref[...]
     turned = jnp.concatenate([-tap_t[HALF:], tap_t[:HALF]], axis=0)
     col = lane_iota(1, KPAD)
     second = col >= KROWS // 2
@@ -71,10 +71,6 @@
     for shift in range(8):
         band_hi[shift * CH : (shift + 1) * CH, :] = roll(wide_hi, shift).astype(BF16)
         band_lo[shift * CH : (shift + 1) * CH, :] = roll(wide_lo, shift).astype(BF16)
-    m = lax.broadcasted_iota(jnp.int32, (TROWS, TROWS), 0)
-    tap = jnp.where(m < 272, (m & 15) * KI + (m >> 4), jnp.where(m < 289, 16 * KI + m - 272, -1))
-    pick = (lane_iota(TROWS, TROWS) == tap).astype(F32)
-    compact_ref[...] = mm_exact(pick, taps)
 
 
 def shifted(left, centre, right, s, lane):
@@ -129,21 +125,46 @@
         s_lo[48 * k : 48 * k + 48, 512:640] = low
 
 
-def invert(t):
-    lane = lane_iota(HALF)
-    sub = lax.broadcasted_iota(jnp.int32, (HALF, LANES), 0)
-    lane_row = lane_iota(1)
-    for k in range(HALF):
-        pivot = 1.0 / t[k : k + 1, k : k + 1]
-        row = t[k : k + 1, :]
-        row = jnp.where(lane_row == k, 1.0, jnp.where(lane_row == HALF + k, 0.0, row)) * pivot
-        other = jnp.where(lane_row < HALF, -roll(row, HALF), roll(row, HALF))
-        here = sub == k
-        real = jnp.where(here, -1.0, t[:, k : k + 1])
-        imag = jnp.where(here, 0.0, t[:, HALF + k : HALF + k + 1])
-        kept = jnp.where(here | (lane == k) | (lane == HALF + k), 0.0, t)
-        t = kept - real * row - imag * other
-    return t
+def invert(matrix):
+    shape = (8, LANES)
+    lane = lane_iota(8)
+    pair = (lane & (HALF - 1)) >> 1
+    sub = lax.broadcasted_iota(jnp.int32, shape, 0)
+    turn = jnp.where(lane < HALF, -1.0, 1.0)
+    tiles = [matrix[8 * v : 8 * v + 8] for v in range(HALF // 8)]
+
+    def fill(value):
+        return jnp.broadcast_to(value, shape)
+
+    for k in range(0, HALF, 2):
+        v, r = divmod(k, 8)
+        row1, row2 = fill(tiles[v][r : r + 1, :]), fill(tiles[v][r + 1 : r + 2, :])
+        a, d = fill(row1[:, k : k + 1]), fill(row2[:, k + 1 : k + 2])
+        br, bi = fill(row1[:, k + 1 : k + 2]), fill(row1[:, HALF + k + 1 : HALF + k + 2])
+        cut = pair == k // 2
+        row1 = jnp.where(cut, jnp.where(lane == k, 1.0, 0.0), row1)
+        row2 = jnp.where(cut, jnp.where(lane == k + 1, 1.0, 0.0), row2)
+        turned1, turned2 = roll(row1, HALF) * turn, roll(row2, HALF) * turn
+        p1 = 1.0 / a
+        er, ei = br * p1, bi * p1
+        p2 = 1.0 / (d - (br * er + bi * ei))
+        new2 = p2 * (row2 - (er * row1 - ei * turned1))
+        spun2 = p2 * (turned2 - (er * turned1 + ei * row1))
+        new1 = p1 * row1 - (er * new2 + ei * spun2)
+        spun1 = p1 * turned1 - (er * spun2 - ei * new2)
+        after = []
+        for w, tile in enumerate(tiles):
+            first = fill(tile[:, k : k + 1]) * new1 + fill(tile[:, HALF + k : HALF + k + 1]) * spun1
+            second = (
+                fill(tile[:, k + 1 : k + 2]) * new2
+                + fill(tile[:, HALF + k + 1 : HALF + k + 2]) * spun2
+            )
+            value = jnp.where(cut, 0.0, tile) - (first + second)
+            if w == v:
+                value = jnp.where(sub == r, new1, jnp.where(sub == r + 1, new2, value))
+            after.append(value)
+        tiles = after
+    return jnp.concatenate(tiles, axis=0)
 
 
 def counts(start, length, total, index):
@@ -151,33 +172,34 @@
     return (jnp.minimum(at + HW, total - 1) - jnp.maximum(at - HW, 0) + 1).astype(F32)
 
 
-def kernel(
+def gather_kernel(
     n_inl,
     n_xl,
     spectra_ref,
+    omega_hbm,
+    sketch_ref,
+    moments_ref,
+    inverse_ref,
+    y_hi,
+    y_lo,
+    block_ref,
     omega_ref,
-    sketch_out,
-    denoised_ref,
-    block_ref,
     taps_ref,
-    compact_ref,
     band_hi,
     band_lo,
     s_hi,
     s_lo,
-    y_hi,
-    y_lo,
-    sketch_ref,
     prod_ref,
     send_ref,
+    gram_ref,
+    gram_b,
+    gram_part,
+    gram_c,
     recv_a,
     part_ref,
     recv_b,
     full_ref,
     recv_c,
-    spread_ref,
-    c_hi,
-    c_lo,
     halo_send,
     halo_recv,
     a_send,
@@ -186,12 +208,19 @@
     b_recv,
     c_send,
     c_recv,
-    out_sem,
+    gb_send,
+    gb_recv,
+    gc_send,
+    gc_recv,
+    own_sem,
+    omega_sem,
 ):
+    own_copy = pltpu.make_async_copy(spectra_ref, block_ref.at[1, 1], own_sem)
+    own_copy.start()
+    omega_copy = pltpu.make_async_copy(omega_hbm, omega_ref, omega_sem)
+    omega_copy.start()
     inl = lax.axis_index("inl")
     xl = lax.axis_index("xl")
-    share = TROWS // n_inl
-
     up, down = inl > 0, inl < n_inl - 1
     west, east = xl > 0, xl < n_xl - 1
     barrier = pltpu.get_barrier_semaphore()
@@ -251,10 +280,10 @@
         def _(dr=dr, dc=dc):
             block_ref[1 + dr, 1 + dc] = jnp.zeros((2, 16, LANES), F32)
 
-    block_ref[1, 1] = spectra_ref[...]
-
-    prepare_weights(omega_ref, taps_ref, compact_ref, band_hi, band_lo)
-
+    omega_copy.wait()
+    prepare_weights(omega_ref, taps_ref, band_hi, band_lo)
+
+    own_copy.wait()
     for n, (dr, dc) in enumerate(sides):
 
         @pl.when(exists(dr, dc))
@@ -283,8 +312,63 @@
         y_hi[shift * CH : (shift + 1) * CH, 128:384] = high
         y_lo[shift * CH : (shift + 1) * CH, 128:384] = low
 
-    copy_out = pltpu.make_async_copy(sketch_ref, sketch_out, out_sem)
-    copy_out.start()
+    sums = None
+    for shift in range(8):
+        rows = slice(shift * CH, (shift + 1) * CH)
+        high = y_hi[rows, 128:384]
+        term = mm_t(jnp.concatenate([high, y_lo[rows, 128:384]], axis=0), high)
+        sums = term if sums is None else sums + term
+    sign = jnp.where(lane_iota(1) < HALF, 1.0, -1.0)
+    products = sums[:CH] + (sums[CH:] + sums[CH:].T)
+    gram = products[:HALF] + roll(products[HALF:], HALF) * sign
+    lane = lane_iota(HALF)
+    sub = lax.broadcasted_iota(jnp.int32, (HALF, LANES), 0)
+    gram = jnp.where(sub >= lane, gram, roll(gram, HALF))
+    gram_ref[...] = jnp.where(lane[:32] < HALF, gram[:32], roll(gram[32:], HALF))
+
+    def piece(at):
+        share = TROWS // n_inl
+        return pl.ds(pl.multiple_of(at * share, 8), share)
+
+    def exchange(axis, source, slots, sems):
+        me, count = (inl, n_inl) if axis == "inl" else (xl, n_xl)
+        send, recv = sems
+        pieces = source.shape[0] != slots.shape[1]
+
+        def copy(k):
+            peer = lax.rem(me + k, count)
+            return pltpu.make_async_remote_copy(
+                src_ref=source.at[piece(peer)] if pieces else source,
+                dst_ref=slots.at[me],
+                send_sem=send.at[k],
+                recv_sem=recv.at[k],
+                device_id={axis: peer},
+                device_id_type=MESH,
+            )
+
+        def start():
+            for k in range(1, count):
+                copy(k).start()
+            slots[me] = source[piece(me), :] if pieces else source[...]
+
+        def wait():
+            for k in range(1, count):
+                copy(k).wait()
+
+        return start, wait
+
+    def summed(slots):
+        values = [slots[k] for k in range(slots.shape[0])]
+        while len(values) > 1:
+            values = [a + b for a, b in zip(values[::2], values[1::2])]
+        return values[0]
+
+    gram_xl = exchange("xl", gram_ref, gram_b, (gb_send, gb_recv))
+    gram_inl = exchange("inl", gram_part, gram_c, (gc_send, gc_recv))
+    scatter_inl = exchange("inl", send_ref, recv_a, (a_send, a_recv))
+    across_xl = exchange("xl", part_ref, recv_b, (b_send, b_recv))
+    gather_inl = exchange("inl", full_ref, recv_c, (c_send, c_recv))
+    gram_xl[0]()
 
     main_hi, main_lo = s_hi[0:KROWS, 128:384], s_lo[0:KROWS, 128:384]
     prod_ref[KROWS : KROWS + 8, :] = jnp.zeros((8, 256), F32)
@@ -301,98 +385,81 @@
     prod_ref[0:KROWS, 0:LANES] = total
     first = prod_ref[0 : KROWS // 2, 0:LANES]
     second = prod_ref[KROWS // 2 : KROWS, 0:LANES]
-    sign = jnp.where(lane_iota(1) < HALF, 1.0, -1.0)
     moments = roll(second, HALF) + first * sign
     for q in range(KI):
         send_ref[q * 16 : q * 16 + 16, :] = moments[q * WIN : q * WIN + 16]
         send_ref[272 + q : 273 + q, :] = moments[q * WIN + 16 : q * WIN + 17]
     send_ref[289:TROWS, :] = jnp.zeros((TROWS - 289, LANES), F32)
 
-    def piece(at):
-        return pl.ds(pl.multiple_of(at * share, 8), share)
-
-    def scatter(k):
-        peer = lax.rem(inl + k, n_inl)
-        return pltpu.make_async_remote_copy(
-            src_ref=send_ref.at[piece(peer)],
-            dst_ref=recv_a.at[inl],
-            send_sem=a_send.at[k],
-            recv_sem=a_recv.at[k],
-            device_id={"inl": peer},
-            device_id_type=MESH,
-        )
-
-    def across(k):
-        return pltpu.make_async_remote_copy(
-            src_ref=part_ref,
-            dst_ref=recv_b.at[xl],
-            send_sem=b_send.at[k],
-            recv_sem=b_recv.at[k],
-            device_id={"xl": lax.rem(xl + k, n_xl)},
-            device_id_type=MESH,
-        )
-
-    def gather(k):
-        return pltpu.make_async_remote_copy(
-            src_ref=full_ref,
-            dst_ref=recv_c.at[inl],
-            send_sem=c_send.at[k],
-            recv_sem=c_recv.at[k],
-            device_id={"inl": lax.rem(inl + k, n_inl)},
-            device_id_type=MESH,
-        )
-
-    for k in range(1, n_inl):
-        scatter(k).start()
-    recv_a[inl] = send_ref[piece(inl), :]
+    scatter_inl[0]()
 
     build_side(block_ref, s_hi, s_lo)
+
     side_lane = lane_iota(1)
     keep_up = up.astype(F32)
     keep_down = down.astype(F32)
-    keep_side = jnp.where(side_lane % 16 < 8, west.astype(F32), east.astype(F32))
+    keep_side = jnp.where(side_lane % 16 < 8, west.astype(F32), east.astype(F32)) * jnp.where(
+        side_lane < 16, keep_up, jnp.where((side_lane >= 48) & (side_lane < 64), keep_down, 1.0)
+    )
     keep = jnp.concatenate([jnp.full((1, LANES), keep_down), keep_side], axis=1)
-    for shift in range(8):
+
+    def outer_rows(shift):
         rows = slice(shift * CH, (shift + 1) * CH)
         high, low = split(sketch_rows(shift, 0, LANES) * keep_up)
         y_hi[rows, 0:128] = high
         y_lo[rows, 0:128] = low
-        value = sketch_rows(shift, 384, 256)
-        side = value[:, LANES:]
-        side_keep = jnp.where(
-            side_lane < 16, keep_up, jnp.where((side_lane >= 48) & (side_lane < 64), keep_down, 1.0)
-        )
-        high, low = split(value * keep * jnp.concatenate([jnp.ones((1, LANES), F32), side_keep], axis=1))
+        high, low = split(sketch_rows(shift, 384, 256) * keep)
         y_hi[rows, 384:640] = high
         y_lo[rows, 384:640] = low
 
-    for k in range(1, n_inl):
-        scatter(k).wait()
-    value = recv_a[0]
-    for k in range(1, n_inl):
-        value = value + recv_a[k]
-    part_ref[...] = value
-    for k in range(1, n_xl):
-        across(k).start()
-    recv_b[xl] = value
-    for k in range(1, n_xl):
-        across(k).wait()
-    value = recv_b[0]
-    for k in range(1, n_xl):
-        value = value + recv_b[k]
-    full_ref[...] = value
-    for k in range(1, n_inl):
-        gather(k).start()
-    recv_c[inl] = value
-    for k in range(1, n_inl):
-        gather(k).wait()
-
-    moments = recv_c[...].reshape(TROWS, LANES)
-    products = mm_exact(moments.T, compact_ref[...])
-    gram = products[:HALF] - roll(products[HALF:], HALF) * sign
-    inverse = invert(gram)
+    for shift in range(4):
+        outer_rows(shift)
+    gram_xl[1]()
+    gram_part[...] = summed(gram_b)
+    gram_inl[0]()
+    for shift in range(4, 8):
+        outer_rows(shift)
+    scatter_inl[1]()
+    part_ref[...] = summed(recv_a)
+    across_xl[0]()
+    gram_inl[1]()
+    packed = summed(gram_c)
+    packed = jnp.concatenate([packed, roll(packed, HALF)], axis=0)
+    flipped = jnp.concatenate([packed, jnp.zeros_like(packed)], axis=0).T[:HALF]
+    real = jnp.where(sub >= lane, packed, flipped)
+    imag = jnp.where(sub < lane, packed, jnp.where(sub > lane, -flipped, 0.0))
+    gram = jnp.where(lane < HALF, real, roll(imag, HALF))
+    across_xl[1]()
+    full_ref[...] = summed(recv_b)
+    gather_inl[0]()
+    inverse_ref[...] = invert(gram)
+    gather_inl[1]()
+    moments_ref[...] = recv_c[...].reshape(TROWS, LANES)
+
+
+def spread_kernel(
+    n_inl,
+    n_xl,
+    sketch_ref,
+    moments_ref,
+    inverse_ref,
+    y_hi,
+    y_lo,
+    sketch_out,
+    denoised_ref,
+    spread_ref,
+    c_hi,
+    c_lo,
+    out_sem,
+):
+    inl = lax.axis_index("inl")
+    xl = lax.axis_index("xl")
+    copy_out = pltpu.make_async_copy(sketch_ref, sketch_out, out_sem)
+    copy_out.start()
+    sign = jnp.where(lane_iota(1) < HALF, 1.0, -1.0)
+    inverse = inverse_ref[...]
     mixing = jnp.concatenate([inverse * sign, roll(inverse, HALF)], axis=0)
-    coeffs = mm_exact(moments, mixing)
+    coeffs = mm_exact(moments_ref[...], mixing)
 
     spread_ref[:, 0:8, :] = jnp.zeros((GROUPS, 8, LANES), F32)
     spread_ref[:, 24:32, :] = jnp.zeros((GROUPS, 8, LANES), F32)
@@ -420,6 +487,7 @@
         term = roll(term, 16 * (window - 2))
         edge = term if edge is None else edge + term
 
+    copy_out.wait()
     lane = lane_iota(8)
     sub = lax.broadcasted_iota(jnp.int32, (8, LANES), 0)
     count_j = counts(xl * LANES, LANES, n_xl * LANES, lane)
@@ -437,56 +505,80 @@
             count_i = counts(inl * 16 + 8 * h, 16, n_inl * 16, sub)
             denoised_ref[x, 8 * h : 8 * h + 8, :] = total / (count_i * count_j)
 
-    copy_out.wait()
-
 
 def per_device(n_inl, n_xl, spectra, omega):
-    share = TROWS // n_inl
     vmem = pltpu.VMEM
     dma = pltpu.SemaphoreType.DMA
-    sketch, denoised = pl.pallas_call(
-        functools.partial(kernel, n_inl, n_xl),
+    here = pl.BlockSpec(memory_space=pltpu.VMEM)
+    anywhere = pl.BlockSpec(memory_space=pl.ANY)
+    limit = 24 * 1024 * 1024
+
+    share = TROWS // n_inl
+    inl_sems = [dma((n_inl,))] * 2
+    xl_sems = [dma((n_xl,))] * 2
+    results = pl.pallas_call(
+        functools.partial(gather_kernel, n_inl, n_xl),
         out_shape=(
             jax.ShapeDtypeStruct((CH * 16, LANES), F32),
-            jax.ShapeDtypeStruct((2, 16, LANES), F32),
+            jax.ShapeDtypeStruct((TROWS, LANES), F32),
+            jax.ShapeDtypeStruct((HALF, LANES), F32),
+            jax.ShapeDtypeStruct((8 * CH, 640), BF16),
+            jax.ShapeDtypeStruct((8 * CH, 640), BF16),
         ),
-        in_specs=[pl.BlockSpec(memory_space=pltpu.VMEM)] * 2,
-        out_specs=(pl.BlockSpec(memory_space=pl.ANY), pl.BlockSpec(memory_space=pltpu.VMEM)),
+        in_specs=[pl.BlockSpec(memory_space=pltpu.HBM)] * 2,
+        out_specs=(here,) * 5,
         scratch_shapes=[
             vmem((3, 3, 2, 16, LANES), F32),
-            vmem((TROWS, LANES), F32),
-            vmem((TROWS, LANES), F32),
+            vmem((2, HALF, KI * KI), F32),
+            vmem((CH, TROWS), F32),
             vmem((8 * CH, KPAD), BF16),
             vmem((8 * CH, KPAD), BF16),
             vmem((KPAD, 640), BF16),
             vmem((KPAD, 640), BF16),
-            vmem((8 * CH, 640), BF16),
-            vmem((8 * CH, 640), BF16),
-            vmem((CH * 16, LANES), F32),
             vmem((KROWS + 8, 256), F32),
             vmem((TROWS, LANES), F32),
+            vmem((32, LANES), F32),
+            vmem((n_xl, 32, LANES), F32),
+            vmem((32, LANES), F32),
+            vmem((n_inl, 32, LANES), F32),
             vmem((n_inl, share, LANES), F32),
             vmem((share, LANES), F32),
             vmem((n_xl, share, LANES), F32),
             vmem((share, LANES), F32),
             vmem((n_inl, share, LANES), F32),
+            dma((8,)),
+            dma((8,)),
+            *inl_sems,
+            *xl_sems,
+            *inl_sems,
+            *xl_sems,
+            *inl_sems,
+            dma,
+            dma,
+        ],
+        compiler_params=pltpu.CompilerParams(
+            collective_id=0, has_side_effects=True, vmem_limit_bytes=limit
+        ),
+    )(
+        pltpu.with_memory_space_constraint(spectra[0], pltpu.HBM),
+        pltpu.with_memory_space_constraint(omega.transpose(0, 2, 1), pltpu.HBM),
+    )
+    sketch, denoised = pl.pallas_call(
+        functools.partial(spread_kernel, n_inl, n_xl),
+        out_shape=(
+            jax.ShapeDtypeStruct((CH * 16, LANES), F32),
+            jax.ShapeDtypeStruct((2, 16, LANES), F32),
+        ),
+        in_specs=[anywhere] + [here] * 4,
+        out_specs=(anywhere, here),
+        scratch_shapes=[
             vmem((GROUPS, 32, LANES), F32),
             vmem((GROUPS * 8, 8 * LANES), BF16),
             vmem((GROUPS * 8, 8 * LANES), BF16),
-            dma((8,)),
-            dma((8,)),
-            dma((n_inl,)),
-            dma((n_inl,)),
-            dma((n_xl,)),
-            dma((n_xl,)),
-            dma((n_inl,)),
-            dma((n_inl,)),
             dma,
         ],
-        compiler_params=pltpu.CompilerParams(
-            collective_id=0, has_side_effects=True, vmem_limit_bytes=48 * 1024 * 1024
-        ),
-    )(spectra[0], omega)
+        compiler_params=pltpu.CompilerParams(vmem_limit_bytes=limit),
+    )(*results)
     return sketch.reshape(1, CH, 16, LANES), denoised[None]
 
 

time: 52.1 us -> 47.3 us (0.908)
  local copies, waits for them, and re-layouts: 2.66 us -> 0 us
  Pallas kernels: 48.7 us -> 46.4 us
    unnamed x5 -> x0, local copies, waits for them, and re-layouts: 2.66 us -> none
    pallas_call x1 -> x2, Pallas kernels: 48.7 us -> 46.4 us  [the longest x1 41.7 us: per_device(): pl.pallas_call(functools.partial(gather_kernel, n_inl, n_xl), out_shape=(...]
where the time goes in v1:
time: 47.3 us; the launch traced here: 47.2 us
  Pallas kernels  46.4 us (98%)
  between operations  0.8 us (2%)
    pallas_call x1, Pallas kernels, per_device(): pl.pallas_call(functools.partial(gather_kernel, n_inl, n_xl), out_shape=(...  41.7 us
    pallas_call x1, Pallas kernels, per_device(): pl.pallas_call(functools.partial(spread_kernel, n_inl, n_xl), out_shape=(...  4.66 us

profile of v1, /device:TPU:8, one launch (start us, length us, event | category | flops | bytes accessed | tf_op | source)
XLA Modules:
  0.0 47.2 jit_solution(11096903722698512491)
XLA Ops:
  0.6 41.7 %shard_map.41 = (f32[2048,128]{1,0:T(8,128)S(1)}, f32[384,128]{1,0:T(8,128)S(1)}, f32[64,128]{1,0:T(8,128)S(1)}, bf16[1024,640]{1,0:T(8,128)(2,1)S(1)}, bf16[1024,640]{1,0:T(8,128)(2,1)S(1)}) custom-call(f32[2,16,128]{2,1,0:T(8,128)} %bitcast.5, f32[2,64,289]{2,1,0:T(8,128)} %bitcast.4), custom_call_target="tpu_custom_call" | custom-call | tf_op jit(solution)/shard_map/pallas_call | solution.py:519
  42.4 4.7 %shard_map.42 = (f32[2048,128]{1,0:T(8,128)}, f32[2,16,128]{2,1,0:T(8,128)}) custom-call(f32[2048,128]{1,0:T(8,128)S(1)} %get-tuple-element.9.sketch_ref, f32[384,128]{1,0:T(8,128)S(1)} %get-tuple-element.10.moments_ref, f32[64,128]{1,0:T(8,128)S(1)} %get-tuple-element.11.inverse_ref, bf16[1024,640]{1,0:T(8,128)(2,1)S(1)} %get-tuple-element.12.y_hi, ...), custom_call_target="tpu_custom_call" | custom-call | tf_op jit(solution)/shard_map/pallas_call | solution.py:566

commit v2 on v1

--- a/solution.py
+++ b/solution.py
@@ -195,6 +195,7 @@
     gram_b,
     gram_part,
     gram_c,
+    matrix_ref,
     recv_a,
     part_ref,
     recv_b,
@@ -234,14 +235,15 @@
                 ok = one if ok is None else ok & one
         return ok
 
-    for k in range(1, n_inl):
-        pl.semaphore_signal(
-            barrier, inc=1, device_id={"inl": lax.rem(inl + k, n_inl)}, device_id_type=MESH
-        )
-    for k in range(1, n_xl):
-        pl.semaphore_signal(
-            barrier, inc=1, device_id={"xl": lax.rem(xl + k, n_xl)}, device_id_type=MESH
-        )
+    def greet(axis, steps):
+        me, count = (inl, n_inl) if axis == "inl" else (xl, n_xl)
+        for k in steps:
+            pl.semaphore_signal(
+                barrier, inc=1, device_id={axis: lax.rem(me + k, count)}, device_id_type=MESH
+            )
+
+    greet("inl", sorted({1, n_inl - 1}))
+    greet("xl", sorted({1, n_xl - 1}))
     expected = n_inl - 1 + n_xl - 1
     for dr, dc in sides:
         if dr != 0 and dc != 0:
@@ -254,6 +256,8 @@
                     barrier, inc=1, device_id={"inl": inl + dr, "xl": xl + dc}, device_id_type=MESH
                 )
 
+    greet("inl", range(2, n_inl - 1))
+    greet("xl", range(2, n_xl - 1))
     s_hi[KROWS:KPAD, :] = jnp.zeros((KPAD - KROWS, 640), BF16)
     s_lo[KROWS:KPAD, :] = jnp.zeros((KPAD - KROWS, 640), BF16)
     pl.semaphore_wait(barrier, expected)
@@ -294,37 +298,11 @@
         def _(n=n, dr=dr, dc=dc):
             halo(n, dr, dc).wait_recv()
 
-    build_main(block_ref, s_hi, s_lo)
-
     def sketch_rows(shift, at, width):
         rows = slice(shift * CH, (shift + 1) * CH)
         left_hi = band_hi[rows, :]
         right = s_hi[:, at : at + width]
         return mm(left_hi, right) + mm(band_lo[rows, :], right) + mm(left_hi, s_lo[:, at : at + width])
-
-    for shift in range(8):
-        value = sketch_rows(shift, LANES, 2 * LANES)
-        for half in range(2):
-            sketch_ref[pl.ds(8 * half + shift, CH, stride=16), :] = value[
-                :, half * LANES : (half + 1) * LANES
-            ]
-        high, low = split(value)
-        y_hi[shift * CH : (shift + 1) * CH, 128:384] = high
-        y_lo[shift * CH : (shift + 1) * CH, 128:384] = low
-
-    sums = None
-    for shift in range(8):
-        rows = slice(shift * CH, (shift + 1) * CH)
-        high = y_hi[rows, 128:384]
-        term = mm_t(jnp.concatenate([high, y_lo[rows, 128:384]], axis=0), high)
-        sums = term if sums is None else sums + term
-    sign = jnp.where(lane_iota(1) < HALF, 1.0, -1.0)
-    products = sums[:CH] + (sums[CH:] + sums[CH:].T)
-    gram = products[:HALF] + roll(products[HALF:], HALF) * sign
-    lane = lane_iota(HALF)
-    sub = lax.broadcasted_iota(jnp.int32, (HALF, LANES), 0)
-    gram = jnp.where(sub >= lane, gram, roll(gram, HALF))
-    gram_ref[...] = jnp.where(lane[:32] < HALF, gram[:32], roll(gram[32:], HALF))
 
     def piece(at):
         share = TROWS // n_inl
@@ -368,73 +346,122 @@
     scatter_inl = exchange("inl", send_ref, recv_a, (a_send, a_recv))
     across_xl = exchange("xl", part_ref, recv_b, (b_send, b_recv))
     gather_inl = exchange("inl", full_ref, recv_c, (c_send, c_recv))
-    gram_xl[0]()
-
-    main_hi, main_lo = s_hi[0:KROWS, 128:384], s_lo[0:KROWS, 128:384]
-    prod_ref[KROWS : KROWS + 8, :] = jnp.zeros((8, 256), F32)
-    total = None
-    for pair in range(4):
-        rows = slice(pair * 256, (pair + 1) * 256)
-        own_hi = y_hi[rows, 128:384]
-        prod_ref[0:KROWS, :] = (
-            mm_t(main_hi, own_hi) + mm_t(main_lo, own_hi) + mm_t(main_hi, y_lo[rows, 128:384])
+
+    stage = pl.loop(0, 1 + jnp.minimum(inl, 0))
+
+    @stage
+    def _(_once):
+        build_main(block_ref, s_hi, s_lo)
+        sums = None
+        for shift in range(8):
+            value = sketch_rows(shift, LANES, 2 * LANES)
+            for half in range(2):
+                sketch_ref[pl.ds(8 * half + shift, CH, stride=16), :] = value[
+                    :, half * LANES : (half + 1) * LANES
+                ]
+            high, low = split(value)
+            y_hi[shift * CH : (shift + 1) * CH, 128:384] = high
+            y_lo[shift * CH : (shift + 1) * CH, 128:384] = low
+            term = mm_t(jnp.concatenate([high, low], axis=0), high)
+            sums = term if sums is None else sums + term
+        sign = jnp.where(lane_iota(1) < HALF, 1.0, -1.0)
+        products = sums[:CH] + (sums[CH:] + sums[CH:].T)
+        gram = products[:HALF] + roll(products[HALF:], HALF) * sign
+        lane = lane_iota(HALF)
+        sub = lax.broadcasted_iota(jnp.int32, (HALF, LANES), 0)
+        gram = jnp.where(sub >= lane, gram, roll(gram, HALF))
+        gram_ref[...] = jnp.where(lane[:32] < HALF, gram[:32], roll(gram[32:], HALF))
+        gram_xl[0]()
+
+    @stage
+    def _(_once):
+        main_hi, main_lo = s_hi[0:KROWS, 128:384], s_lo[0:KROWS, 128:384]
+        prod_ref[KROWS : KROWS + 8, :] = jnp.zeros((8, 256), F32)
+        total = None
+        for pair in range(4):
+            rows = slice(pair * 256, (pair + 1) * 256)
+            own_hi = y_hi[rows, 128:384]
+            prod_ref[0:KROWS, :] = (
+                mm_t(main_hi, own_hi) + mm_t(main_lo, own_hi) + mm_t(main_hi, y_lo[rows, 128:384])
+            )
+            for k in range(2):
+                term = prod_ref[2 * pair + k : 2 * pair + k + KROWS, k * LANES : (k + 1) * LANES]
+                total = term if total is None else total + term
+        prod_ref[0:KROWS, 0:LANES] = total
+        first = prod_ref[0 : KROWS // 2, 0:LANES]
+        second = prod_ref[KROWS // 2 : KROWS, 0:LANES]
+        sign = jnp.where(lane_iota(1) < HALF, 1.0, -1.0)
+        moments = roll(second, HALF) + first * sign
+        for q in range(KI):
+            send_ref[q * 16 : q * 16 + 16, :] = moments[q * WIN : q * WIN + 16]
+            send_ref[272 + q : 273 + q, :] = moments[q * WIN + 16 : q * WIN + 17]
+        send_ref[289:TROWS, :] = jnp.zeros((TROWS - 289, LANES), F32)
+        scatter_inl[0]()
+
+    def outer_rows(shifts):
+        side_lane = lane_iota(1)
+        keep_up = up.astype(F32)
+        keep_down = down.astype(F32)
+        keep_side = jnp.where(side_lane % 16 < 8, west.astype(F32), east.astype(F32)) * jnp.where(
+            side_lane < 16, keep_up, jnp.where((side_lane >= 48) & (side_lane < 64), keep_down, 1.0)
         )
-        for k in range(2):
-            term = prod_ref[2 * pair + k : 2 * pair + k + KROWS, k * LANES : (k + 1) * LANES]
-            total = term if total is None else total + term
-    prod_ref[0:KROWS, 0:LANES] = total
-    first = prod_ref[0 : KROWS // 2, 0:LANES]
-    second = prod_ref[KROWS // 2 : KROWS, 0:LANES]
-    moments = roll(second, HALF) + first * sign
-    for q in range(KI):
-        send_ref[q * 16 : q * 16 + 16, :] = moments[q * WIN : q * WIN + 16]
-        send_ref[272 + q : 273 + q, :] = moments[q * WIN + 16 : q * WIN + 17]
-    send_ref[289:TROWS, :] = jnp.zeros((TROWS - 289, LANES), F32)
-
-    scatter_inl[0]()
-
-    build_side(block_ref, s_hi, s_lo)
-
-    side_lane = lane_iota(1)
-    keep_up = up.astype(F32)
-    keep_down = down.astype(F32)
-    keep_side = jnp.where(side_lane % 16 < 8, west.astype(F32), east.astype(F32)) * jnp.where(
-        side_lane < 16, keep_up, jnp.where((side_lane >= 48) & (side_lane < 64), keep_down, 1.0)
-    )
-    keep = jnp.concatenate([jnp.full((1, LANES), keep_down), keep_side], axis=1)
-
-    def outer_rows(shift):
-        rows = slice(shift * CH, (shift + 1) * CH)
-        high, low = split(sketch_rows(shift, 0, LANES) * keep_up)
-        y_hi[rows, 0:128] = high
-        y_lo[rows, 0:128] = low
-        high, low = split(sketch_rows(shift, 384, 256) * keep)
-        y_hi[rows, 384:640] = high
-        y_lo[rows, 384:640] = low
-
-    for shift in range(4):
-        outer_rows(shift)
-    gram_xl[1]()
-    gram_part[...] = summed(gram_b)
-    gram_inl[0]()
-    for shift in range(4, 8):
-        outer_rows(shift)
-    scatter_inl[1]()
-    part_ref[...] = summed(recv_a)
-    across_xl[0]()
-    gram_inl[1]()
-    packed = summed(gram_c)
-    packed = jnp.concatenate([packed, roll(packed, HALF)], axis=0)
-    flipped = jnp.concatenate([packed, jnp.zeros_like(packed)], axis=0).T[:HALF]
-    real = jnp.where(sub >= lane, packed, flipped)
-    imag = jnp.where(sub < lane, packed, jnp.where(sub > lane, -flipped, 0.0))
-    gram = jnp.where(lane < HALF, real, roll(imag, HALF))
-    across_xl[1]()
-    full_ref[...] = summed(recv_b)
-    gather_inl[0]()
-    inverse_ref[...] = invert(gram)
-    gather_inl[1]()
-    moments_ref[...] = recv_c[...].reshape(TROWS, LANES)
+        keep = jnp.concatenate([jnp.full((1, LANES), keep_down), keep_side], axis=1)
+        for shift in shifts:
+            rows = slice(shift * CH, (shift + 1) * CH)
+            high, low = split(sketch_rows(shift, 0, LANES) * keep_up)
+            y_hi[rows, 0:128] = high
+            y_lo[rows, 0:128] = low
+            high, low = split(sketch_rows(shift, 384, 256) * keep)
+            y_hi[rows, 384:640] = high
+            y_lo[rows, 384:640] = low
+
+    @stage
+    def _(_once):
+        build_side(block_ref, s_hi, s_lo)
+        outer_rows(range(4))
+
+    @stage
+    def _(_once):
+        gram_xl[1]()
+        gram_part[...] = summed(gram_b)
+        gram_inl[0]()
+
+    @stage
+    def _(_once):
+        outer_rows(range(4, 8))
+
+    @stage
+    def _(_once):
+        scatter_inl[1]()
+        part_ref[...] = summed(recv_a)
+        across_xl[0]()
+
+    @stage
+    def _(_once):
+        gram_inl[1]()
+        packed = summed(gram_c)
+        packed = jnp.concatenate([packed, roll(packed, HALF)], axis=0)
+        flipped = jnp.concatenate([packed, jnp.zeros_like(packed)], axis=0).T[:HALF]
+        lane = lane_iota(HALF)
+        sub = lax.broadcasted_iota(jnp.int32, (HALF, LANES), 0)
+        real = jnp.where(sub >= lane, packed, flipped)
+        imag = jnp.where(sub < lane, packed, jnp.where(sub > lane, -flipped, 0.0))
+        matrix_ref[...] = jnp.where(lane < HALF, real, roll(imag, HALF))
+
+    @stage
+    def _(_once):
+        across_xl[1]()
+        full_ref[...] = summed(recv_b)
+        gather_inl[0]()
+
+    @stage
+    def _(_once):
+        inverse_ref[...] = invert(matrix_ref[...])
+
+    @stage
+    def _(_once):
+        gather_inl[1]()
+        moments_ref[...] = recv_c[...].reshape(TROWS, LANES)
 
 
 def spread_kernel(
@@ -541,6 +568,7 @@
             vmem((n_xl, 32, LANES), F32),
             vmem((32, LANES), F32),
             vmem((n_inl, 32, LANES), F32),
+            vmem((HALF, LANES), F32),
             vmem((n_inl, share, LANES), F32),
             vmem((share, LANES), F32),
             vmem((n_xl, share, LANES), F32),

time: 47.3 us -> 41.9 us (0.89)
  Pallas kernels: 46.4 us -> 40.9 us
    pallas_call x1, Pallas kernels: 41.7 us -> 36.3 us  [per_device(): pl.pallas_call(functools.partial(gather_kernel, n_inl, n_xl), out_shape=(...]
where the time goes in v2:
time: 41.9 us; the launch traced here: 41.7 us
  Pallas kernels  40.9 us (98%)
  between operations  0.8 us (2%)
    pallas_call x1, Pallas kernels, per_device(): pl.pallas_call(functools.partial(gather_kernel, n_inl, n_xl), out_shape=(...  36.3 us
    pallas_call x1, Pallas kernels, per_device(): pl.pallas_call(functools.partial(spread_kernel, n_inl, n_xl), out_shape=(...  4.66 us

profile of v2, /device:TPU:8, one launch (start us, length us, event | category | flops | bytes accessed | tf_op | source)
XLA Modules:
  0.0 41.7 jit_solution(6295106229234967658)
XLA Ops:
  0.6 36.3 %shard_map.41 = (f32[2048,128]{1,0:T(8,128)S(1)}, f32[384,128]{1,0:T(8,128)S(1)}, f32[64,128]{1,0:T(8,128)S(1)}, bf16[1024,640]{1,0:T(8,128)(2,1)S(1)}, bf16[1024,640]{1,0:T(8,128)(2,1)S(1)}) custom-call(f32[2,16,128]{2,1,0:T(8,128)} %bitcast.5, f32[2,64,289]{2,1,0:T(8,128)} %bitcast.4), custom_call_target="tpu_custom_call" | custom-call | tf_op jit(solution)/shard_map/pallas_call | solution.py:546
  36.9 4.7 %shard_map.42 = (f32[2048,128]{1,0:T(8,128)}, f32[2,16,128]{2,1,0:T(8,128)}) custom-call(f32[2048,128]{1,0:T(8,128)S(1)} %get-tuple-element.9.sketch_ref, f32[384,128]{1,0:T(8,128)S(1)} %get-tuple-element.10.moments_ref, f32[64,128]{1,0:T(8,128)S(1)} %get-tuple-element.11.inverse_ref, bf16[1024,640]{1,0:T(8,128)(2,1)S(1)} %get-tuple-element.12.y_hi, ...), custom_call_target="tpu_custom_call" | custom-call | tf_op jit(solution)/shard_map/pallas_call | solution.py:594

commit v3 on v2

--- a/solution.py
+++ b/solution.py
@@ -29,10 +29,6 @@
 
 def mm(a, b):
     return jnp.dot(a, b, preferred_element_type=F32)
-
-
-def mm_exact(a, b):
-    return jnp.dot(a, b, preferred_element_type=F32, precision=lax.Precision.HIGHEST)
 
 
 def mm_t(a, b):
@@ -412,8 +408,10 @@
             y_hi[rows, 0:128] = high
             y_lo[rows, 0:128] = low
             high, low = split(sketch_rows(shift, 384, 256) * keep)
-            y_hi[rows, 384:640] = high
-            y_lo[rows, 384:640] = low
+            y_hi[rows, 384:512] = high[:, :LANES]
+            y_lo[rows, 384:512] = low[:, :LANES]
+            rest = roll(low[:, LANES:].astype(F32), HALF)
+            y_hi[rows, 512:640] = jnp.where(side_lane < HALF, high[:, LANES:].astype(F32), rest).astype(BF16)
 
     @stage
     def _(_once):
@@ -475,8 +473,7 @@
     sketch_out,
     denoised_ref,
     spread_ref,
-    c_hi,
-    c_lo,
+    c_both,
     out_sem,
 ):
     inl = lax.axis_index("inl")
@@ -486,7 +483,9 @@
     sign = jnp.where(lane_iota(1) < HALF, 1.0, -1.0)
     inverse = inverse_ref[...]
     mixing = jnp.concatenate([inverse * sign, roll(inverse, HALF)], axis=0)
-    coeffs = mm_exact(moments_ref[...], mixing)
+    mixing_hi, mixing_lo = split(mixing)
+    high, low = split(moments_ref[...])
+    coeffs = mm(high, mixing_hi) + mm(low, mixing_hi) + mm(high, mixing_lo)
 
     spread_ref[:, 0:8, :] = jnp.zeros((GROUPS, 8, LANES), F32)
     spread_ref[:, 24:32, :] = jnp.zeros((GROUPS, 8, LANES), F32)
@@ -495,22 +494,23 @@
             spread_ref[x * KI + q, 8:24, :] = value[q * 16 : q * 16 + 16]
             spread_ref[x * KI + q, 24:25, :] = value[272 + q : 273 + q]
 
+    size = GROUPS * 8
     main = None
     edge = None
     for window in range(3):
         for shift in range(8):
             at = 8 + 8 * window - shift
-            value = spread_ref[:, at : at + 8, :].reshape(GROUPS * 8, LANES)
+            value = spread_ref[:, at : at + 8, :].reshape(size, LANES)
             high, low = split(value)
-            c_hi[:, shift * LANES : (shift + 1) * LANES] = high
-            c_lo[:, shift * LANES : (shift + 1) * LANES] = low
-        high, low = c_hi[...], c_lo[...]
+            c_both[0:size, shift * LANES : (shift + 1) * LANES] = high
+            c_both[size : 2 * size, shift * LANES : (shift + 1) * LANES] = low
+        both = c_both[...]
         at = (2 - window) * LANES
-        y = y_hi[:, at : at + 256]
-        term = mm(high, y) + mm(low, y) + mm(high, y_lo[:, at : at + 256])
+        term = mm(both, y_hi[:, at : at + 256])
+        term = term[:size] + term[size:] + mm(both[:size], y_lo[:, at : at + 256])
         main = term if main is None else main + term
-        y = y_hi[:, 512:640]
-        term = mm(high, y) + mm(low, y) + mm(high, y_lo[:, 512:640])
+        term = mm(both, y_hi[:, 512:640])
+        term = term[:size] + roll(term[:size], HALF) + term[size:]
         term = roll(term, 16 * (window - 2))
         edge = term if edge is None else edge + term
 
@@ -550,7 +550,7 @@
             jax.ShapeDtypeStruct((TROWS, LANES), F32),
             jax.ShapeDtypeStruct((HALF, LANES), F32),
             jax.ShapeDtypeStruct((8 * CH, 640), BF16),
-            jax.ShapeDtypeStruct((8 * CH, 640), BF16),
+            jax.ShapeDtypeStruct((8 * CH, 512), BF16),
         ),
         in_specs=[pl.BlockSpec(memory_space=pltpu.HBM)] * 2,
         out_specs=(here,) * 5,
@@ -601,8 +601,7 @@
         out_specs=(anywhere, here),
         scratch_shapes=[
             vmem((GROUPS, 32, LANES), F32),
-            vmem((GROUPS * 8, 8 * LANES), BF16),
-            vmem((GROUPS * 8, 8 * LANES), BF16),
+            vmem((2 * GROUPS * 8, 8 * LANES), BF16),
             dma,
         ],
         compiler_params=pltpu.CompilerParams(vmem_limit_bytes=limit),

time: 41.9 us -> 41.8 us (level)
  no operation moved by 1% of the time
where the time goes in v3:
time: 41.8 us; the launch traced here: 41.6 us
  Pallas kernels  40.8 us (98%)
  between operations  0.8 us (2%)
    pallas_call x1, Pallas kernels, per_device(): pl.pallas_call(functools.partial(gather_kernel, n_inl, n_xl), out_shape=(...  36.2 us
    pallas_call x1, Pallas kernels, per_device(): pl.pallas_call(functools.partial(spread_kernel, n_inl, n_xl), out_shape=(...  4.6 us

profile of v3, /device:TPU:8, one launch (start us, length us, event | category | flops | bytes accessed | tf_op | source)
XLA Modules:
  0.0 41.6 jit_solution(8965504244868460048)
XLA Ops:
  0.6 36.2 %shard_map.41 = (f32[2048,128]{1,0:T(8,128)S(1)}, f32[384,128]{1,0:T(8,128)S(1)}, f32[64,128]{1,0:T(8,128)S(1)}, bf16[1024,640]{1,0:T(8,128)(2,1)S(1)}, bf16[1024,512]{1,0:T(8,128)(2,1)S(1)}) custom-call(f32[2,16,128]{2,1,0:T(8,128)} %bitcast.5, f32[2,64,289]{2,1,0:T(8,128)} %bitcast.4), custom_call_target="tpu_custom_call" | custom-call | tf_op jit(solution)/shard_map/pallas_call | solution.py:546
  36.8 4.6 %shard_map.42 = (f32[2048,128]{1,0:T(8,128)}, f32[2,16,128]{2,1,0:T(8,128)}) custom-call(f32[2048,128]{1,0:T(8,128)S(1)} %get-tuple-element.9.sketch_ref, f32[384,128]{1,0:T(8,128)S(1)} %get-tuple-element.10.moments_ref, f32[64,128]{1,0:T(8,128)S(1)} %get-tuple-element.11.inverse_ref, bf16[1024,640]{1,0:T(8,128)(2,1)S(1)} %get-tuple-element.12.y_hi, ...), custom_call_target="tpu_custom_call" | custom-call | tf_op jit(solution)/shard_map/pallas_call | solution.py:594

commit v4 on v3

--- a/solution.py
+++ b/solution.py
@@ -221,7 +221,7 @@
     up, down = inl > 0, inl < n_inl - 1
     west, east = xl > 0, xl < n_xl - 1
     barrier = pltpu.get_barrier_semaphore()
-    sides = [(dr, dc) for dr in (-1, 0, 1) for dc in (-1, 0, 1) if (dr, dc) != (0, 0)]
+    sides = [(-1, -1), (-1, 1), (1, -1), (1, 1), (-1, 0), (1, 0), (0, -1), (0, 1)]
 
     def exists(dr, dc):
         ok = None
@@ -320,8 +320,15 @@
                 device_id_type=MESH,
             )
 
+        def hops(k):
+            if axis == "xl":
+                return min(k, count - k)
+            return min(k // 4, count // 4 - k // 4) + min(k % 4, 4 - k % 4)
+
+        far_first = sorted(range(1, count), key=hops, reverse=True)
+
         def start():
-            for k in range(1, count):
+            for k in far_first:
                 copy(k).start()
             slots[me] = source[piece(me), :] if pieces else source[...]
 
@@ -426,13 +433,13 @@
 
     @stage
     def _(_once):
-        outer_rows(range(4, 8))
-
-    @stage
-    def _(_once):
         scatter_inl[1]()
         part_ref[...] = summed(recv_a)
         across_xl[0]()
+
+    @stage
+    def _(_once):
+        outer_rows(range(4, 8))
 
     @stage
     def _(_once):

time: 41.8 us -> 41.5 us (level)
  Pallas kernels: 40.8 us -> 40.3 us
    pallas_call x1, Pallas kernels: 36.2 us -> 35.7 us  [per_device(): pl.pallas_call(functools.partial(gather_kernel, n_inl, n_xl), out_shape=(...]
where the time goes in v4:
time: 41.5 us; the launch traced here: 41.1 us
  Pallas kernels  40.3 us (97%)
  between operations  0.8 us (2%)
    pallas_call x1, Pallas kernels, per_device(): pl.pallas_call(functools.partial(gather_kernel, n_inl, n_xl), out_shape=(...  35.7 us
    pallas_call x1, Pallas kernels, per_device(): pl.pallas_call(functools.partial(spread_kernel, n_inl, n_xl), out_shape=(...  4.6 us

profile of v4, /device:TPU:8, one launch (start us, length us, event | category | flops | bytes accessed | tf_op | source)
XLA Modules:
  0.0 41.1 jit_solution(9191206001393069372)
XLA Ops:
  0.6 35.7 %shard_map.41 = (f32[2048,128]{1,0:T(8,128)S(1)}, f32[384,128]{1,0:T(8,128)S(1)}, f32[64,128]{1,0:T(8,128)S(1)}, bf16[1024,640]{1,0:T(8,128)(2,1)S(1)}, bf16[1024,512]{1,0:T(8,128)(2,1)S(1)}) custom-call(f32[2,16,128]{2,1,0:T(8,128)} %bitcast.5, f32[2,64,289]{2,1,0:T(8,128)} %bitcast.4), custom_call_target="tpu_custom_call" | custom-call | tf_op jit(solution)/shard_map/pallas_call | solution.py:553
  36.3 4.6 %shard_map.42 = (f32[2048,128]{1,0:T(8,128)}, f32[2,16,128]{2,1,0:T(8,128)}) custom-call(f32[2048,128]{1,0:T(8,128)S(1)} %get-tuple-element.9.sketch_ref, f32[384,128]{1,0:T(8,128)S(1)} %get-tuple-element.10.moments_ref, f32[64,128]{1,0:T(8,128)S(1)} %get-tuple-element.11.inverse_ref, bf16[1024,640]{1,0:T(8,128)(2,1)S(1)} %get-tuple-element.12.y_hi, ...), custom_call_target="tpu_custom_call" | custom-call | tf_op jit(solution)/shard_map/pallas_call | solution.py:601

commit v5 on v4

--- a/solution.py
+++ b/solution.py
@@ -502,21 +502,23 @@
             spread_ref[x * KI + q, 24:25, :] = value[272 + q : 273 + q]
 
     size = GROUPS * 8
-    main = None
-    edge = None
     for window in range(3):
         for shift in range(8):
             at = 8 + 8 * window - shift
             value = spread_ref[:, at : at + 8, :].reshape(size, LANES)
             high, low = split(value)
-            c_both[0:size, shift * LANES : (shift + 1) * LANES] = high
-            c_both[size : 2 * size, shift * LANES : (shift + 1) * LANES] = low
-        both = c_both[...]
-        at = (2 - window) * LANES
-        term = mm(both, y_hi[:, at : at + 256])
-        term = term[:size] + term[size:] + mm(both[:size], y_lo[:, at : at + 256])
-        main = term if main is None else main + term
-        term = mm(both, y_hi[:, 512:640])
+            lanes = slice((8 * window + shift) * LANES, (8 * window + shift + 1) * LANES)
+            c_both[0:size, lanes] = high
+            c_both[size : 2 * size, lanes] = low
+
+    def stacked(ref):
+        return jnp.concatenate([ref[:, at : at + 256] for at in (2 * LANES, LANES, 0)], axis=0)
+
+    main = mm(c_both[...], stacked(y_hi))
+    main = main[:size] + main[size:] + mm(c_both[0:size, :], stacked(y_lo))
+    edge = None
+    for window in range(3):
+        term = mm(c_both[:, 1024 * window : 1024 * (window + 1)], y_hi[:, 512:640])
         term = term[:size] + roll(term[:size], HALF) + term[size:]
         term = roll(term, 16 * (window - 2))
         edge = term if edge is None else edge + term
@@ -608,7 +610,7 @@
         out_specs=(anywhere, here),
         scratch_shapes=[
             vmem((GROUPS, 32, LANES), F32),
-            vmem((2 * GROUPS * 8, 8 * LANES), BF16),
+            vmem((2 * GROUPS * 8, 24 * LANES), BF16),
             dma,
         ],
         compiler_params=pltpu.CompilerParams(vmem_limit_bytes=limit),

time: 41.5 us -> 40.8 us (0.983)
  Pallas kernels: 40.3 us -> 39.6 us
    pallas_call x1, Pallas kernels: 4.6 us -> 3.9 us  [per_device(): pl.pallas_call(functools.partial(spread_kernel, n_inl, n_xl), out_shape=(...]
where the time goes in v5:
time: 40.8 us; the launch traced here: 40.4 us
  Pallas kernels  39.6 us (97%)
  between operations  0.8 us (2%)
    pallas_call x1, Pallas kernels, per_device(): pl.pallas_call(functools.partial(gather_kernel, n_inl, n_xl), out_shape=(...  35.7 us
    pallas_call x1, Pallas kernels, per_device(): pl.pallas_call(functools.partial(spread_kernel, n_inl, n_xl), out_shape=(...  3.9 us

profile of v5, /device:TPU:8, one launch (start us, length us, event | category | flops | bytes accessed | tf_op | source)
XLA Modules:
  0.0 40.4 jit_solution(4267555169259571836)
XLA Ops:
  0.6 35.7 %shard_map.41 = (f32[2048,128]{1,0:T(8,128)S(1)}, f32[384,128]{1,0:T(8,128)S(1)}, f32[64,128]{1,0:T(8,128)S(1)}, bf16[1024,640]{1,0:T(8,128)(2,1)S(1)}, bf16[1024,512]{1,0:T(8,128)(2,1)S(1)}) custom-call(f32[2,16,128]{2,1,0:T(8,128)} %bitcast.5, f32[2,64,289]{2,1,0:T(8,128)} %bitcast.4), custom_call_target="tpu_custom_call" | custom-call | tf_op jit(solution)/shard_map/pallas_call | solution.py:555
  36.3 3.9 %shard_map.42 = (f32[2048,128]{1,0:T(8,128)}, f32[2,16,128]{2,1,0:T(8,128)}) custom-call(f32[2048,128]{1,0:T(8,128)S(1)} %get-tuple-element.9.sketch_ref, f32[384,128]{1,0:T(8,128)S(1)} %get-tuple-element.10.moments_ref, f32[64,128]{1,0:T(8,128)S(1)} %get-tuple-element.11.inverse_ref, bf16[1024,640]{1,0:T(8,128)(2,1)S(1)} %get-tuple-element.12.y_hi, ...), custom_call_target="tpu_custom_call" | custom-call | tf_op jit(solution)/shard_map/pallas_call | solution.py:603
